TPU v7x, 32 devices: a whole 2x2x4 slice. The times are simulated.
32 devices in a mesh: illum: 2 (over y), slab: 16 (over z, x, core).
Axes of the slice: x: 2, y: 2, z: 4, core: 2. Of those that a mesh axis runs over, the one named last changes fastest.
Arguments:
- incident: bfloat16 [2, 2, 64, 256, 128], P('illum', None, 'slab'), may hold values from -6 to 6
- field_now: float32 [2, 2, 64, 256, 128], P('illum', None, 'slab'), may hold values from -6 to 6
- contrast: float32 [64, 256, 128], P('slab'), may hold values from 0 to 0.5
- green_spectrum: float32 [2, 64, 256, 128], P(None, None, 'slab'), may hold values from -6 to 6
- detector_data: float32 [2, 2, 256, 128], P('illum', None, 'slab'), may hold values from -6 to 6
Outputs:
- field_next: float32 [2, 2, 64, 256, 128], P('illum', None, 'slab')
- misfit: float32 [2, 2, 256, 128], P('illum', None, 'slab')
- contrast_next: float32 [64, 256, 128], P('slab')
All inputs are finite; a program needn't handle non-finite values.
Results may differ from a plain program's by a relative error of at most 0.0003.
Values sent between devices are 32-bit elements; how exact they have to be, the bound alone decides.
A program may use at most 64 MiB of HBM per device.

v0:
```python
import math

import jax
import jax.numpy as jnp
import ml_dtypes
import numpy as np
from jax import lax
from jax.experimental import pallas as pl
from jax.experimental.pallas import tpu as pltpu
from jax.sharding import PartitionSpec as P

wave_number = 1.2
step_size = 2.0
diffusion = 0.02
edge_scale = 0.25
passes = 4
MESH = pl.DeviceIdType.MESH
highest = lax.Precision.HIGH
form_rows = "...xy,xk->...ky"
form_cols = "...y,yk->...k"
form_depth = "azxy,zk->akxy"


def with_halo(array, sides, width):
    for axis, dim in sides:
        devices, length = (lax.axis_size(axis), array.shape[dim])
        up = [(i, (i + 1) % devices) for i in range(devices - 1)]
        down = [(j, i) for i, j in up]
        last = lax.slice_in_dim(array, length - width, length, axis=dim)
        leading = lax.slice_in_dim(array, 0, width, axis=dim)
        before = lax.ppermute(last, axis, up)
        after = lax.ppermute(leading, axis, down)
        array = jnp.concatenate([before, array, after], axis=dim)
    return array


def tables(length):
    counter = jnp.arange(length, dtype=jnp.int32)
    product = counter[:, None] * counter[None, :] % length
    angle = product.astype(jnp.float32) * (2.0 * math.pi / length)
    scale = 1.0 / math.sqrt(length)
    return (jnp.cos(angle) * scale, jnp.sin(angle) * scale)


def mixing(real, imag, cosine, sine_table, sign, form):
    real_cos = jnp.einsum(form, real, cosine, precision=highest)
    real_sin = jnp.einsum(form, real, sine_table, precision=highest)
    imag_cos = jnp.einsum(form, imag, cosine, precision=highest)
    imag_sin = jnp.einsum(form, imag, sine_table, precision=highest)
    return (real_cos - sign * imag_sin, imag_cos + sign * real_sin)


def frequency(index, length):
    shifted = jnp.where(index < length // 2, index, index - length)
    return shifted.astype(jnp.float32) * (2.0 * math.pi / length)


def propagator(depth_index, row_index, width_x, width_y, depth):
    along_x = frequency(row_index, width_x)
    along_y = frequency(jnp.arange(width_y, dtype=jnp.int32), width_y)
    squared = wave_number**2 - along_x[None, :, None] ** 2 - along_y[None, None, :] ** 2
    distance = (depth - depth_index).astype(jnp.float32)[:, None, None]
    root = jnp.sqrt(jnp.abs(squared))
    moving = squared > 0.0
    amplitude = jnp.where(moving, 1.0, jnp.exp(-root * distance))
    phase = jnp.where(moving, root * distance, 0.0)
    return (amplitude * jnp.cos(phase), amplitude * jnp.sin(phase))


def tv_pass(padded, first, depth):
    rows = padded.shape[0]
    global_row = first + jnp.arange(rows - 1, dtype=jnp.int32)
    inside = (global_row >= 0) & (global_row <= depth - 2)
    core = padded[:-1]
    slope_depth = jnp.where(inside[:, None, None], padded[1:] - core, 0.0)
    slope_rows = jnp.concatenate([core[:, 1:] - core[:, :-1], jnp.zeros_like(core[:, :1])], axis=1)
    slope_cols = jnp.concatenate(
        [core[:, :, 1:] - core[:, :, :-1], jnp.zeros_like(core[:, :, :1])], axis=2
    )
    magnitude = jnp.sqrt(slope_depth**2 + slope_rows**2 + slope_cols**2 + edge_scale**2)
    flux_depth = slope_depth / magnitude
    flux_rows = (slope_rows / magnitude)[1:]
    flux_cols = (slope_cols / magnitude)[1:]
    spread_depth = flux_depth[1:] - flux_depth[:-1]
    spread_rows = flux_rows - jnp.concatenate(
        [jnp.zeros_like(flux_rows[:, :1]), flux_rows[:, :-1]], axis=1
    )
    spread_cols = flux_cols - jnp.concatenate(
        [jnp.zeros_like(flux_cols[:, :, :1]), flux_cols[:, :, :-1]], axis=2
    )
    return padded[1:-1] + diffusion * (spread_depth + spread_rows + spread_cols)


def back_project(prop_real, prop_imag, mismatch, root_depth):
    miss_real = mismatch[:, 0][:, None]
    miss_imag = mismatch[:, 1][:, None]
    out_real = (prop_real[None] * miss_real + prop_imag[None] * miss_imag) / root_depth
    out_imag = (prop_real[None] * miss_imag - prop_imag[None] * miss_real) / root_depth
    return jnp.stack([out_real, out_imag], 1)


def shards(incident, field_now, contrast, green_spectrum, detector_data):
    slabs = lax.axis_size("slab")
    place = lax.axis_index("slab")
    local_depth, width_x, width_y = contrast.shape
    depth = local_depth * slabs
    cols_x = width_x // slabs
    root_depth = math.sqrt(depth)
    cos_x, sin_x = tables(width_x)
    cos_y, sin_y = tables(width_y)
    cos_z, sin_z = tables(depth)
    real_now = field_now[:, 0]
    imag_now = field_now[:, 1]
    spec_real, spec_imag = mixing(
        contrast[None] * real_now, contrast[None] * imag_now, cos_x, sin_x, -1.0, form_rows
    )
    spec_real, spec_imag = mixing(spec_real, spec_imag, cos_y, sin_y, -1.0, form_cols)
    spectrum = jnp.stack([spec_real, spec_imag], 1)
    columns = lax.all_to_all(spectrum, "slab", split_axis=3, concat_axis=2, tiled=True)
    deep_real, deep_imag = mixing(columns[:, 0], columns[:, 1], cos_z, sin_z, -1.0, form_depth)
    green_real = green_spectrum[0][None]
    green_imag = green_spectrum[1][None]
    prod_real = green_real * deep_real - green_imag * deep_imag
    prod_imag = green_real * deep_imag + green_imag * deep_real
    vol_real, vol_imag = mixing(prod_real, prod_imag, cos_z, sin_z, 1.0, form_depth)
    volume = jnp.stack([vol_real, vol_imag], 1)
    kx_index = place * cols_x + jnp.arange(cols_x, dtype=jnp.int32)
    col_prop_real, col_prop_imag = propagator(
        jnp.arange(depth, dtype=jnp.int32), kx_index, width_x, width_y, depth
    )
    col_real = columns[:, 0]
    col_imag = columns[:, 1]
    pred_real = (
        jnp.sum(col_prop_real[None] * col_real - col_prop_imag[None] * col_imag, axis=1)
        / root_depth
    )
    pred_imag = (
        jnp.sum(col_prop_real[None] * col_imag + col_prop_imag[None] * col_real, axis=1)
        / root_depth
    )
    mismatch = jnp.stack([pred_real, pred_imag], 1) - detector_data
    volume = lax.all_to_all(volume, "slab", split_axis=2, concat_axis=3, tiled=True)
    depth_index = place * local_depth + jnp.arange(local_depth, dtype=jnp.int32)
    prop_real, prop_imag = propagator(
        depth_index, jnp.arange(width_x, dtype=jnp.int32), width_x, width_y, depth
    )
    gathered = lax.all_gather(mismatch, "slab", axis=2, tiled=True)
    returned = back_project(prop_real, prop_imag, gathered, root_depth)
    scat_real, scat_imag = mixing(volume[:, 0], volume[:, 1], cos_x, sin_x, 1.0, form_rows)
    scat_real, scat_imag = mixing(scat_real, scat_imag, cos_y, sin_y, 1.0, form_cols)
    field_next = incident.astype(jnp.float32) + jnp.stack([scat_real, scat_imag], 1)
    ret_real, ret_imag = mixing(returned[:, 0], returned[:, 1], cos_x, sin_x, 1.0, form_rows)
    ret_real, ret_imag = mixing(ret_real, ret_imag, cos_y, sin_y, 1.0, form_cols)
    local_terms = jnp.sum(real_now * ret_real + imag_now * ret_imag, axis=0)
    illums = lax.axis_size("illum")
    gradient, travelling = local_terms, local_terms
    for hop in range(illums - 1):
        travelling = lax.ppermute(travelling, "illum", [(i, (i + 1) % illums) for i in range(illums)])
        gradient = gradient + travelling
    updated = contrast - step_size * gradient
    wide = math.gcd(passes, local_depth)
    for repeat in range(passes // wide):
        updated = with_halo(updated, (("slab", 0),), wide)
        for left in range(wide, 0, -1):
            updated = tv_pass(updated, place * local_depth - left, depth)
    return (field_next, mismatch, updated)


def split_halves(value):
    high = value.astype(jnp.bfloat16)
    return high, (value - high.astype(jnp.float32)).astype(jnp.bfloat16)


def product(left, right):
    return jnp.dot(left, right, preferred_element_type=jnp.float32)


def combine(both, sign):
    rows, cols = both.shape[0] // 2, both.shape[1] // 2
    by_cos, by_sin = both[:rows], both[rows:]
    real = by_cos[:, :cols] - sign * by_sin[:, cols:]
    imag = by_cos[:, cols:] + sign * by_sin[:, :cols]
    return real, imag


def transform_rows(pair, high_ref, low_ref, sign):
    high, low = split_halves(pair)
    table = high_ref[...]
    both = product(table, high) + product(table, low) + product(low_ref[...], high)
    return jnp.concatenate(combine(both, sign), axis=1)


def transform_cols(pair, high_ref, low_ref):
    high, low = split_halves(pair)
    table = high_ref[...]
    return product(high, table) + product(low, table) + product(high, low_ref[...])


def host_split(table):
    table = table.astype(np.float32)
    high = table.astype(ml_dtypes.bfloat16)
    low = (table - high.astype(np.float32)).astype(ml_dtypes.bfloat16)
    return high, low


def host_tables(length):
    counter = np.arange(length)
    angle = (counter[:, None] * counter[None, :] % length) * (2.0 * math.pi / length)
    return np.cos(angle) / math.sqrt(length), np.sin(angle) / math.sqrt(length)


def host_frequency(length):
    index = np.arange(length)
    return np.where(index < length // 2, index, index - length) * (2.0 * math.pi / length)


def host_propagator(distance, width_x, width_y):
    squared = (
        wave_number**2 - host_frequency(width_x)[:, None] ** 2 - host_frequency(width_y)[None] ** 2
    )
    root = np.sqrt(np.abs(squared))
    moving = squared > 0.0
    amplitude = np.where(moving, 1.0, np.exp(-root * distance))
    phase = np.where(moving, root * distance, 0.0)
    pair = [amplitude * np.cos(phase), amplitude * np.sin(phase)]
    return np.concatenate(pair, axis=1).astype(np.float32)


def fused_kernel(
    field, contrast, detector, xh, xl, yfh, yfl, yih, yil, zt_ref, step_ref,
    incident_any, green_any, start_any,
    field_out, misfit_out, contrast_out,
    out1, in1, out2, in2, miss, gmine, gpeer, cube, cube2, zbuf, gbuf, rbuf, fz, inc, green, start,
    load_sem, s1, r1, s2, r2, sm, rm, sg, rg, sh, rh,
):
    slabs, local_depth, cols_x, pair_y = out1.shape
    width_y = pair_y // 2
    width_x = slabs * cols_x
    depth = slabs * local_depth
    root_depth = math.sqrt(depth)
    me = lax.axis_index("slab")
    lane = lax.axis_index("illum")
    other = 1 - lane

    def at(hop):
        return lax.rem(me + hop, slabs)

    def spread(body):
        lax.fori_loop(1, slabs, lambda hop, carry: (body(at(hop)), carry)[1], 0)

    barrier = pltpu.get_barrier_semaphore()

    def greet(dst):
        pl.semaphore_signal(barrier, inc=1, device_id=(lane, dst), device_id_type=MESH)

    spread(greet)
    pl.semaphore_signal(barrier, inc=1, device_id=(other, me), device_id_type=MESH)
    loads = [
        pltpu.make_async_copy(green_any, green, load_sem.at[0]),
        pltpu.make_async_copy(start_any.at[me], start, load_sem.at[1]),
        pltpu.make_async_copy(incident_any, inc, load_sem.at[2]),
    ]
    for load in loads:
        load.start()

    def remote(src, dst, send, recv, who):
        return pltpu.make_async_remote_copy(
            src_ref=src, dst_ref=dst, send_sem=send, recv_sem=recv,
            device_id=who, device_id_type=MESH,
        )

    def forward(plane, carry):
        c = contrast[plane]
        pair = jnp.concatenate([c * field[0, 0, plane], c * field[0, 1, plane]], axis=1)
        pair = transform_cols(pair, yfh, yfl)
        pair = transform_rows(pair, xh, xl, -1.0)
        out1[:, plane] = pair.reshape(slabs, cols_x, pair_y)
        return carry

    groups = math.gcd(local_depth, 2)
    size = local_depth // groups
    for group in range(groups):
        lax.fori_loop(group * size, (group + 1) * size, forward, 0)
        if group == 0:
            pl.semaphore_wait(barrier, slabs)
        part = pl.ds(group * size, size)
        spread(
            lambda dst: remote(
                out1.at[dst, part], in1.at[me, part], s1.at[dst], r1.at[me], (lane, dst)
            ).start()
        )
    in1[me] = out1[me]

    loads[0].wait()
    loads[1].wait()
    loads[2].wait()
    for first in range(0, cols_x, 8):
        rows = slice(first, first + 8)
        for half in range(2):
            cols = slice(half * width_y, (half + 1) * width_y)
            gbuf[rows, :, cols] = jnp.transpose(green[half, :, rows, :], (1, 0, 2))

    def arrived(src):
        remote(out1.at[src], in1.at[src], s1.at[src], r1.at[src], (lane, src)).wait_recv()

    spread(arrived)
    own = pl.ds(pl.multiple_of(me * cols_x, cols_x), cols_x)
    step_r, step_i = step_ref[own, :width_y], step_ref[own, width_y:]

    def horner(src, carry):
        real, imag = carry
        for plane in range(local_depth):
            real = real + in1[src, plane, :, :width_y]
            imag = imag + in1[src, plane, :, width_y:]
            real, imag = (real * step_r - imag * step_i, real * step_i + imag * step_r)
        return real, imag

    zero = jnp.zeros((cols_x, width_y), jnp.float32)
    real, imag = lax.fori_loop(0, slabs, horner, (zero, zero))
    real = real / root_depth - detector[0, 0]
    imag = imag / root_depth - detector[0, 1]
    misfit_out[0, 0] = real
    misfit_out[0, 1] = imag
    miss[me, :, :width_y] = real
    miss[me, :, width_y:] = imag
    spread(
        lambda dst: remote(miss.at[me], miss.at[me], sm.at[dst], rm.at[me], (lane, dst)).start()
    )

    for first in range(0, cols_x, 8):
        rows = slice(first, first + 8)
        block = in1[:, :, rows, :].reshape(depth, 8, pair_y)
        zbuf[rows] = jnp.transpose(block, (1, 0, 2))

    def convolve(row, carry):
        table = zt_ref[...]
        high, low = split_halves(zbuf[row])
        both = product(table, jnp.concatenate([high, low, high], axis=0))
        real, imag = combine(both, -1.0)
        g_real, g_imag = gbuf[row, :, :width_y], gbuf[row, :, width_y:]
        pair = jnp.concatenate(
            [g_real * real - g_imag * imag, g_real * imag + g_imag * real], axis=1
        )
        high, low = split_halves(pair)
        both = product(table, jnp.concatenate([high, low, high], axis=0))
        zbuf[row] = jnp.concatenate(combine(both, 1.0), axis=1)
        return carry

    lax.fori_loop(0, cols_x, convolve, 0)
    for first in range(0, cols_x, 8):
        rows = slice(first, first + 8)
        block = jnp.transpose(zbuf[rows], (1, 0, 2))
        out2[:, :, rows, :] = block.reshape(slabs, local_depth, 8, pair_y)
    spread(
        lambda dst: remote(out2.at[dst], in2.at[me], s2.at[dst], r2.at[me], (lane, dst)).start()
    )
    in2[me] = out2[me]

    spread(
        lambda src: remote(
            miss.at[src], miss.at[src], sm.at[src], rm.at[src], (lane, src)
        ).wait_recv()
    )
    gathered = miss[...].reshape(width_x, pair_y)
    m_real, m_imag = gathered[:, :width_y], gathered[:, width_y:]
    p_real, p_imag = start[:, :width_y], start[:, width_y:]
    rbuf[:, :width_y] = (p_real * m_real + p_imag * m_imag) / root_depth
    rbuf[:, width_y:] = (p_real * m_imag - p_imag * m_real) / root_depth

    def peer_copy(plane):
        return remote(
            gmine.at[plane], gpeer.at[plane], sg.at[plane], rg.at[plane], (other, me)
        )

    def project(count, carry):
        plane = local_depth - 1 - count
        now = rbuf[...]
        pair = transform_rows(now, xh, xl, 1.0)
        pair = transform_cols(pair, yih, yil)
        gmine[plane] = field[0, 0, plane] * pair[:, :width_y] + field[0, 1, plane] * pair[:, width_y:]
        peer_copy(plane).start()
        now_r, now_i = now[:, :width_y], now[:, width_y:]
        w_real, w_imag = step_ref[:, :width_y], step_ref[:, width_y:]
        rbuf[:, :width_y] = w_real * now_r + w_imag * now_i
        rbuf[:, width_y:] = w_real * now_i - w_imag * now_r
        return carry

    lax.fori_loop(0, local_depth, project, 0)

    def update(count, carry):
        plane = local_depth - 1 - count
        peer_copy(plane).wait()
        cube[passes + plane] = contrast[plane] - step_size * (gmine[plane] + gpeer[plane])
        return carry

    lax.fori_loop(0, local_depth, update, 0)
    low_side, high_side = pl.ds(0, passes), pl.ds(passes + local_depth, passes)
    up = remote(
        cube.at[pl.ds(local_depth, passes)], cube.at[low_side], sh.at[0], rh.at[0],
        (lane, lax.rem(me + 1, slabs)),
    )
    down = remote(
        cube.at[pl.ds(passes, passes)], cube.at[high_side], sh.at[1], rh.at[1],
        (lane, lax.rem(me + slabs - 1, slabs)),
    )
    has_up, has_down = me < slabs - 1, me > 0
    pl.when(has_up)(up.start)
    pl.when(has_down)(down.start)

    @pl.when(me == 0)
    def _():
        cube[low_side] = jnp.zeros((passes, width_x, width_y), jnp.float32)

    @pl.when(me == slabs - 1)
    def _():
        cube[high_side] = jnp.zeros((passes, width_x, width_y), jnp.float32)

    pl.when(has_up)(up.wait_send)
    pl.when(has_down)(down.wait_send)
    pl.when(has_down)(up.wait_recv)
    pl.when(has_up)(down.wait_recv)

    row_at = lax.broadcasted_iota(jnp.int32, (width_x, width_y), 0)
    col_at = lax.broadcasted_iota(jnp.int32, (width_x, width_y), 1)

    def sweep(source, plane, write):
        cur = source[plane]
        place = me * local_depth - passes + plane
        inside = jnp.where((place >= 0) & (place <= depth - 2), 1.0, 0.0)
        slope_z = (source[plane + 1] - cur) * inside
        flux_x = jnp.where(row_at < width_x - 1, pltpu.roll(cur, width_x - 1, 0) - cur, 0.0)
        flux_y = jnp.where(col_at < width_y - 1, pltpu.roll(cur, width_y - 1, 1) - cur, 0.0)
        scale = lax.rsqrt(slope_z**2 + flux_x**2 + flux_y**2 + edge_scale**2)
        flux_z = slope_z * scale
        if write is not None:
            flux_x = flux_x * scale
            flux_y = flux_y * scale
            total = flux_z - fz[...] + flux_x - pltpu.roll(flux_x, 1, 0)
            total = total + flux_y - pltpu.roll(flux_y, 1, 1)
            write(plane, cur + diffusion * total)
        fz[...] = flux_z

    planes = local_depth + 2 * passes
    for turn in range(passes):
        source, target = (cube, cube2) if turn % 2 == 0 else (cube2, cube)
        sweep(source, turn, None)

        def write(plane, value, turn=turn, target=target):
            if turn == passes - 1:
                contrast_out[plane - passes] = value
            else:
                target[plane] = value

        def one(plane, carry, source=source, write=write):
            sweep(source, plane, write)
            return carry

        lax.fori_loop(turn + 1, planes - 1 - turn, one, 0)

    spread(
        lambda src: remote(
            out2.at[src], in2.at[src], s2.at[src], r2.at[src], (lane, src)
        ).wait_recv()
    )

    def finish(plane, carry):
        pair = in2[:, plane].reshape(width_x, pair_y)
        pair = transform_rows(pair, xh, xl, 1.0)
        pair = transform_cols(pair, yih, yil)
        field_out[0, 0, plane] = inc[0, 0, plane].astype(jnp.float32) + pair[:, :width_y]
        field_out[0, 1, plane] = inc[0, 1, plane].astype(jnp.float32) + pair[:, width_y:]
        return carry

    lax.fori_loop(0, local_depth, finish, 0)

    def drain(dst):
        remote(out1.at[dst], in1.at[me], s1.at[dst], r1.at[me], (lane, dst)).wait_send()
        remote(miss.at[me], miss.at[me], sm.at[dst], rm.at[me], (lane, dst)).wait_send()
        remote(out2.at[dst], in2.at[me], s2.at[dst], r2.at[me], (lane, dst)).wait_send()

    spread(drain)


def fused(incident, field_now, contrast, green_spectrum, detector_data):
    slabs = lax.axis_size("slab")
    local_depth, width_x, width_y = contrast.shape
    depth = local_depth * slabs
    cols_x = width_x // slabs
    pair_y = 2 * width_y
    cos_x, sin_x = host_tables(width_x)
    cos_y, sin_y = host_tables(width_y)
    cos_z, sin_z = host_tables(depth)
    xh, xl = host_split(np.concatenate([cos_x, sin_x], axis=0))
    yfh, yfl = host_split(np.block([[cos_y, -sin_y], [sin_y, cos_y]]))
    yih, yil = host_split(np.block([[cos_y, sin_y], [-sin_y, cos_y]]))
    zh, zl = host_split(np.concatenate([cos_z, sin_z], axis=0))
    zt = np.concatenate([zh, zh, zl], axis=1)
    step = host_propagator(1, width_x, width_y)
    nearest = [depth - (s * local_depth + local_depth - 1) for s in range(slabs)]
    start = np.stack([host_propagator(d, width_x, width_y) for d in nearest])
    vmem, anywhere = pl.BlockSpec(memory_space=pltpu.VMEM), pl.BlockSpec(memory_space=pl.ANY)
    f32 = jnp.float32
    block = pltpu.VMEM((slabs, local_depth, cols_x, pair_y), f32)
    planes = pltpu.VMEM((local_depth, width_x, width_y), f32)
    padded = pltpu.VMEM((local_depth + 2 * passes, width_x, width_y), f32)
    turned = pltpu.VMEM((cols_x, depth, pair_y), f32)
    several = pltpu.SemaphoreType.DMA((slabs,))
    return pl.pallas_call(
        fused_kernel,
        out_shape=(
            jax.ShapeDtypeStruct(field_now.shape, f32),
            jax.ShapeDtypeStruct(detector_data.shape, f32),
            jax.ShapeDtypeStruct(contrast.shape, f32),
        ),
        in_specs=[vmem] * 11 + [anywhere] * 3,
        out_specs=(vmem, vmem, vmem),
        scratch_shapes=[
            block, block, block, block,
            pltpu.VMEM((slabs, cols_x, pair_y), f32),
            planes, planes, padded, padded, turned, turned,
            pltpu.VMEM((width_x, pair_y), f32),
            pltpu.VMEM((width_x, width_y), f32),
            pltpu.VMEM(incident.shape, jnp.bfloat16),
            pltpu.VMEM(green_spectrum.shape, f32),
            pltpu.VMEM((width_x, pair_y), f32),
            pltpu.SemaphoreType.DMA((3,)),
            several, several, several, several, several, several,
            pltpu.SemaphoreType.DMA((local_depth,)),
            pltpu.SemaphoreType.DMA((local_depth,)),
            pltpu.SemaphoreType.DMA((2,)),
            pltpu.SemaphoreType.DMA((2,)),
        ],
        compiler_params=pltpu.CompilerParams(
            collective_id=0, has_side_effects=True, vmem_limit_bytes=48 * 2**20
        ),
    )(
        field_now, contrast, detector_data, xh, xl, yfh, yfl, yih, yil, zt, step,
        incident, green_spectrum, start,
    )


def whole_tiles(mesh, arrays):
    local_depth = arrays[2].shape[0]
    rows = arrays[3].shape[2]
    return (
        mesh.shape["illum"] == 2
        and mesh.shape["slab"] > 1
        and rows % 8 == 0
        and (local_depth * mesh.shape["slab"]) % 16 == 0
        and arrays[2].shape[2] % 128 == 0
        and local_depth >= passes
    )


def solution(mesh):
    placed = (
        P("illum", None, "slab", None, None),
        P("illum", None, "slab", None, None),
        P("slab", None, None),
        P(None, None, "slab", None),
        P("illum", None, "slab", None),
    )

    def pick(*arrays):
        return (fused if whole_tiles(mesh, arrays) else shards)(*arrays)

    return jax.shard_map(
        pick,
        mesh=mesh,
        in_specs=placed,
        out_specs=(
            P("illum", None, "slab", None, None),
            P("illum", None, "slab", None),
            P("slab", None, None),
        ),
        check_vma=False,
    )
```

profile of v0, /device:TPU:9, one launch (start us, length us, event | category | flops | bytes accessed | tf_op | source)
XLA Modules:
  0.0 90.7 jit_solution(5659746250174934600)
XLA Ops:
  0.6 0.0 copy-start
  0.6 1.2 %copy-done = f32[1,2,4,256,128]{4,3,2,1,0:T(8,128)S(1)} copy-done((f32[1,2,4,256,128]{4,3,2,1,0:T(8,128)S(1)}, f32[1,2,4,256,128]{4,3,2,1,0:T(8,128)}, u32[]{:S(2)}) %copy-start) | copy-done | bytes 1048600
  1.9 0.0 copy-start.1
  1.9 1.2 %copy-done.1 = f32[2,64,16,128]{3,2,1,0:T(8,128)S(1)} copy-done((f32[2,64,16,128]{3,2,1,0:T(8,128)S(1)}, f32[2,64,16,128]{3,2,1,0:T(8,128)}, u32[]{:S(2)}) %copy-start.1) | copy-done | bytes 1048600
  3.1 0.0 copy-start.2
  3.1 1.0 %copy-done.2 = f32[4,256,128]{2,1,0:T(8,128)S(1)} copy-done((f32[4,256,128]{2,1,0:T(8,128)S(1)}, f32[4,256,128]{2,1,0:T(8,128)}, u32[]{:S(2)}) %copy-start.2) | copy-done | bytes 524312
  4.1 0.0 copy-start.3
  4.1 1.0 %copy-done.3 = bf16[1,2,4,256,128]{4,3,2,1,0:T(8,128)(2,1)S(1)} copy-done((bf16[1,2,4,256,128]{4,3,2,1,0:T(8,128)(2,1)S(1)}, bf16[1,2,4,256,128]{4,3,2,1,0:T(8,128)(2,1)}, u32[]{:S(2)}) %copy-start.3) | copy-done | bytes 524312
  5.2 0.0 copy-start.4
  5.2 0.9 %copy-done.4 = f32[256,256]{1,0:T(8,128)S(1)} copy-done((f32[256,256]{1,0:T(8,128)S(1)}, f32[256,256]{1,0:T(8,128)}, u32[]{:S(2)}) %copy-start.4) | copy-done | bytes 262168
  6.1 0.0 copy-start.5
  6.1 0.9 %copy-done.5 = bf16[512,256]{1,0:T(8,128)(2,1)S(1)} copy-done((bf16[512,256]{1,0:T(8,128)(2,1)S(1)}, bf16[512,256]{1,0:T(8,128)(2,1)}, u32[]{:S(2)}) %copy-start.5) | copy-done | bytes 262168
  7.1 0.0 copy-start.6
  7.1 0.9 %copy-done.6 = bf16[512,256]{1,0:T(8,128)(2,1)S(1)} copy-done((bf16[512,256]{1,0:T(8,128)(2,1)S(1)}, bf16[512,256]{1,0:T(8,128)(2,1)}, u32[]{:S(2)}) %copy-start.6) | copy-done | bytes 262168
  8.0 0.0 copy-start.7
  8.0 0.9 copy-done.7
  8.9 0.0 copy-start.8
  8.9 0.9 copy-done.8
  9.8 0.0 copy-start.9
  9.8 0.9 copy-done.9
  10.7 0.0 copy-start.10
  10.7 0.9 copy-done.10
  11.6 0.0 copy-start.11
  11.6 0.8 copy-done.11
  12.5 0.0 copy-start.12
  12.5 0.7 copy-done.12
  13.2 75.1 %shard_map.157 = (f32[1,2,4,256,128]{4,3,2,1,0:T(8,128)S(1)}, f32[1,2,16,128]{3,2,1,0:T(8,128)S(1)}, f32[4,256,128]{2,1,0:T(8,128)S(1)}) custom-call(f32[1,2,4,256,128]{4,3,2,1,0:T(8,128)S(1)} %copy-done, f32[4,256,128]{2,1,0:T(8,128)S(1)} %copy-done.2, f32[1,2,16,128]{3,2,1,0:T(8,128)S(1)} %copy-done.12, bf16[512,256]{1,0:T(8,128)(2,1)S(1)} %copy-done.6, ...), custom_call_target="tpu_custom_call" | custom-call | tf_op jit(solution)/shard_map/pallas_call | solution.py:508
  88.3 1.0 %copy.20 = f32[1,2,4,256,128]{4,3,2,1,0:T(8,128)} copy(f32[1,2,4,256,128]{4,3,2,1,0:T(8,128)S(1)} %get-tuple-element.6) | data formatting | bytes 2097152
  89.3 0.6 copy.21
  89.9 0.8 copy.22
Async XLA Ops:
  0.6 1.2 %copy-start = (f32[1,2,4,256,128]{4,3,2,1,0:T(8,128)S(1)}, f32[1,2,4,256,128]{4,3,2,1,0:T(8,128)}, u32[]{:S(2)}) copy-start(f32[1,2,4,256,128]{4,3,2,1,0:T(8,128)} %field.1) | copy-start | bytes 3145732
  1.9 1.2 %copy-start.1 = (f32[2,64,16,128]{3,2,1,0:T(8,128)S(1)}, f32[2,64,16,128]{3,2,1,0:T(8,128)}, u32[]{:S(2)}) copy-start(f32[2,64,16,128]{3,2,1,0:T(8,128)} %green_any.1) | copy-start | bytes 3145732
  3.1 1.0 %copy-start.2 = (f32[4,256,128]{2,1,0:T(8,128)S(1)}, f32[4,256,128]{2,1,0:T(8,128)}, u32[]{:S(2)}) copy-start(f32[4,256,128]{2,1,0:T(8,128)} %contrast.1) | copy-start | bytes 1572868
  4.1 1.0 %copy-start.3 = (bf16[1,2,4,256,128]{4,3,2,1,0:T(8,128)(2,1)S(1)}, bf16[1,2,4,256,128]{4,3,2,1,0:T(8,128)(2,1)}, u32[]{:S(2)}) copy-start(bf16[1,2,4,256,128]{4,3,2,1,0:T(8,128)(2,1)} %incident_any.1) | copy-start | bytes 1572868
  5.2 0.9 %copy-start.4 = (f32[256,256]{1,0:T(8,128)S(1)}, f32[256,256]{1,0:T(8,128)}, u32[]{:S(2)}) copy-start(f32[256,256]{1,0:T(8,128)} %constant.25.clone.step_ref) | copy-start | bytes 786436
  6.1 0.9 %copy-start.5 = (bf16[512,256]{1,0:T(8,128)(2,1)S(1)}, bf16[512,256]{1,0:T(8,128)(2,1)}, u32[]{:S(2)}) copy-start(bf16[512,256]{1,0:T(8,128)(2,1)} %constant.19.clone.xl) | copy-start | bytes 786436
  7.1 0.9 %copy-start.6 = (bf16[512,256]{1,0:T(8,128)(2,1)S(1)}, bf16[512,256]{1,0:T(8,128)(2,1)}, u32[]{:S(2)}) copy-start(bf16[512,256]{1,0:T(8,128)(2,1)} %constant.18.clone.xh) | copy-start | bytes 786436
  8.0 0.9 copy-start.7
  8.9 0.9 copy-start.8
  9.8 0.9 copy-start.9
  10.7 0.9 copy-start.10
  11.6 0.8 copy-start.11
  12.5 0.7 copy-start.12
where the time goes:
time: 91.2 us; the launch traced here: 90.7 us
  Pallas kernels  75.1 us (82%)
  local copies, waits for them, and re-layouts  14.9 us (16%)
    pallas_call x1, Pallas kernels, fused(): pl.pallas_call(fused_kernel, out_shape=(jax.ShapeDtypeStruct(field_now.sh...  75.1 us
    unnamed x29, local copies, waits for them, and re-layouts  14.9 us

commit v1 on v0

--- a/solution.py
+++ b/solution.py
@@ -2,7 +2,6 @@
 
 import jax
 import jax.numpy as jnp
-import ml_dtypes
 import numpy as np
 from jax import lax
 from jax.experimental import pallas as pl
@@ -196,13 +195,6 @@
     return product(high, table) + product(low, table) + product(high, low_ref[...])
 
 
-def host_split(table):
-    table = table.astype(np.float32)
-    high = table.astype(ml_dtypes.bfloat16)
-    low = (table - high.astype(np.float32)).astype(ml_dtypes.bfloat16)
-    return high, low
-
-
 def host_tables(length):
     counter = np.arange(length)
     angle = (counter[:, None] * counter[None, :] % length) * (2.0 * math.pi / length)
@@ -227,10 +219,12 @@
 
 
 def fused_kernel(
-    field, contrast, detector, xh, xl, yfh, yfl, yih, yil, zt_ref, step_ref,
-    incident_any, green_any, start_any,
+    field_any, contrast_any, yf_any, x_any, green_any, step_any,
+    detector_any, z_any, start_any, yi_any, incident_any,
     field_out, misfit_out, contrast_out,
-    out1, in1, out2, in2, miss, gmine, gpeer, cube, cube2, zbuf, gbuf, rbuf, fz, inc, green, start,
+    out1, in1, out2, in2, miss, gmine, gpeer, cube, cube2, zbuf, gbuf, rbuf, fz,
+    field, contrast, yf, xt, green, step_ref, detector, zf, start, yi, inc,
+    yfh, yfl, yih, yil, xh, xl, zt_ref,
     load_sem, s1, r1, s2, r2, sm, rm, sg, rg, sh, rh,
 ):
     slabs, local_depth, cols_x, pair_y = out1.shape
@@ -253,15 +247,20 @@
     def greet(dst):
         pl.semaphore_signal(barrier, inc=1, device_id=(lane, dst), device_id_type=MESH)
 
-    spread(greet)
-    pl.semaphore_signal(barrier, inc=1, device_id=(other, me), device_id_type=MESH)
+    sources = [
+        field_any, contrast_any, yf_any, x_any, green_any, step_any,
+        detector_any, z_any, start_any.at[me], yi_any, incident_any,
+    ]
+    held = [field, contrast, yf, xt, green, step_ref, detector, zf, start, yi, inc]
+    early = 4
     loads = [
-        pltpu.make_async_copy(green_any, green, load_sem.at[0]),
-        pltpu.make_async_copy(start_any.at[me], start, load_sem.at[1]),
-        pltpu.make_async_copy(incident_any, inc, load_sem.at[2]),
+        pltpu.make_async_copy(src, dst, load_sem.at[i])
+        for i, (src, dst) in enumerate(zip(sources, held))
     ]
     for load in loads:
         load.start()
+    spread(greet)
+    pl.semaphore_signal(barrier, inc=1, device_id=(other, me), device_id_type=MESH)
 
     def remote(src, dst, send, recv, who):
         return pltpu.make_async_remote_copy(
@@ -277,90 +276,111 @@
         out1[:, plane] = pair.reshape(slabs, cols_x, pair_y)
         return carry
 
+    for load in loads[:early]:
+        load.wait()
+    yfh[...], yfl[...] = split_halves(yf[...])
+    xh[...], xl[...] = split_halves(xt[...])
+    parts = cols_x // 8
     groups = math.gcd(local_depth, 2)
     size = local_depth // groups
+
+    def send_block(part, first, count):
+        planes, rows = pl.ds(first, count), pl.ds(part * 8, 8)
+        spread(
+            lambda dst: remote(
+                out1.at[dst, planes, rows], in1.at[me, planes, rows],
+                s1.at[part, dst], r1.at[part, me], (lane, dst),
+            ).start()
+        )
+
     for group in range(groups):
         lax.fori_loop(group * size, (group + 1) * size, forward, 0)
         if group == 0:
             pl.semaphore_wait(barrier, slabs)
-        part = pl.ds(group * size, size)
-        spread(
-            lambda dst: remote(
-                out1.at[dst, part], in1.at[me, part], s1.at[dst], r1.at[me], (lane, dst)
-            ).start()
-        )
+        send_block(0, group * size, size)
+    for part in range(1, parts):
+        send_block(part, 0, local_depth)
     in1[me] = out1[me]
 
-    loads[0].wait()
-    loads[1].wait()
-    loads[2].wait()
+    for load in loads[early:]:
+        load.wait()
+    yih[...], yil[...] = split_halves(yi[...])
+    z_high, z_low = split_halves(zf[...])
+    zt_ref[...] = jnp.concatenate([z_high, z_high, z_low, z_low], axis=1)
     for first in range(0, cols_x, 8):
         rows = slice(first, first + 8)
         for half in range(2):
             cols = slice(half * width_y, (half + 1) * width_y)
             gbuf[rows, :, cols] = jnp.transpose(green[half, :, rows, :], (1, 0, 2))
 
-    def arrived(src):
-        remote(out1.at[src], in1.at[src], s1.at[src], r1.at[src], (lane, src)).wait_recv()
-
-    spread(arrived)
-    own = pl.ds(pl.multiple_of(me * cols_x, cols_x), cols_x)
-    step_r, step_i = step_ref[own, :width_y], step_ref[own, width_y:]
-
-    def horner(src, carry):
-        real, imag = carry
-        for plane in range(local_depth):
-            real = real + in1[src, plane, :, :width_y]
-            imag = imag + in1[src, plane, :, width_y:]
-            real, imag = (real * step_r - imag * step_i, real * step_i + imag * step_r)
-        return real, imag
-
-    zero = jnp.zeros((cols_x, width_y), jnp.float32)
-    real, imag = lax.fori_loop(0, slabs, horner, (zero, zero))
-    real = real / root_depth - detector[0, 0]
-    imag = imag / root_depth - detector[0, 1]
-    misfit_out[0, 0] = real
-    misfit_out[0, 1] = imag
-    miss[me, :, :width_y] = real
-    miss[me, :, width_y:] = imag
-    spread(
-        lambda dst: remote(miss.at[me], miss.at[me], sm.at[dst], rm.at[me], (lane, dst)).start()
-    )
-
-    for first in range(0, cols_x, 8):
-        rows = slice(first, first + 8)
-        block = in1[:, :, rows, :].reshape(depth, 8, pair_y)
-        zbuf[rows] = jnp.transpose(block, (1, 0, 2))
-
     def convolve(row, carry):
         table = zt_ref[...]
         high, low = split_halves(zbuf[row])
-        both = product(table, jnp.concatenate([high, low, high], axis=0))
+        both = product(table, jnp.concatenate([high, low, high, low], axis=0))
         real, imag = combine(both, -1.0)
         g_real, g_imag = gbuf[row, :, :width_y], gbuf[row, :, width_y:]
         pair = jnp.concatenate(
             [g_real * real - g_imag * imag, g_real * imag + g_imag * real], axis=1
         )
         high, low = split_halves(pair)
-        both = product(table, jnp.concatenate([high, low, high], axis=0))
+        both = product(table, jnp.concatenate([high, low, high, low], axis=0))
         zbuf[row] = jnp.concatenate(combine(both, 1.0), axis=1)
         return carry
 
-    lax.fori_loop(0, cols_x, convolve, 0)
-    for first in range(0, cols_x, 8):
-        rows = slice(first, first + 8)
+    for part in range(parts):
+        rows, cut = slice(part * 8, part * 8 + 8), pl.ds(part * 8, 8)
+        spread(
+            lambda src: remote(
+                out1.at[src, :, cut], in1.at[src, :, cut],
+                s1.at[part, src], r1.at[part, src], (lane, src),
+            ).wait_recv()
+        )
+        own = pl.ds(pl.multiple_of(me * cols_x + part * 8, 8), 8)
+        step_r, step_i = step_ref[own, :width_y], step_ref[own, width_y:]
+
+        def horner(src, carry):
+            real, imag = carry
+            for plane in range(local_depth):
+                real = real + in1[src, plane, rows, :width_y]
+                imag = imag + in1[src, plane, rows, width_y:]
+                real, imag = (real * step_r - imag * step_i, real * step_i + imag * step_r)
+            return real, imag
+
+        zero = jnp.zeros((8, width_y), jnp.float32)
+        real, imag = lax.fori_loop(0, slabs, horner, (zero, zero))
+        real = real / root_depth - detector[0, 0, rows]
+        imag = imag / root_depth - detector[0, 1, rows]
+        misfit_out[0, 0, rows] = real
+        misfit_out[0, 1, rows] = imag
+        miss[me, rows, :width_y] = real
+        miss[me, rows, width_y:] = imag
+        spread(
+            lambda dst: remote(
+                miss.at[me, cut], miss.at[me, cut],
+                sm.at[part, dst], rm.at[part, me], (lane, dst),
+            ).start()
+        )
+        block = in1[:, :, rows, :].reshape(depth, 8, pair_y)
+        zbuf[rows] = jnp.transpose(block, (1, 0, 2))
+        lax.fori_loop(part * 8, part * 8 + 8, convolve, 0)
         block = jnp.transpose(zbuf[rows], (1, 0, 2))
         out2[:, :, rows, :] = block.reshape(slabs, local_depth, 8, pair_y)
-    spread(
-        lambda dst: remote(out2.at[dst], in2.at[me], s2.at[dst], r2.at[me], (lane, dst)).start()
-    )
+        spread(
+            lambda dst: remote(
+                out2.at[dst, :, cut], in2.at[me, :, cut],
+                s2.at[part, dst], r2.at[part, me], (lane, dst),
+            ).start()
+        )
     in2[me] = out2[me]
 
-    spread(
-        lambda src: remote(
-            miss.at[src], miss.at[src], sm.at[src], rm.at[src], (lane, src)
-        ).wait_recv()
-    )
+    for part in range(parts):
+        cut = pl.ds(part * 8, 8)
+        spread(
+            lambda src: remote(
+                miss.at[src, cut], miss.at[src, cut],
+                sm.at[part, src], rm.at[part, src], (lane, src),
+            ).wait_recv()
+        )
     gathered = miss[...].reshape(width_x, pair_y)
     m_real, m_imag = gathered[:, :width_y], gathered[:, width_y:]
     p_real, p_imag = start[:, :width_y], start[:, width_y:]
@@ -457,11 +477,14 @@
 
         lax.fori_loop(turn + 1, planes - 1 - turn, one, 0)
 
-    spread(
-        lambda src: remote(
-            out2.at[src], in2.at[src], s2.at[src], r2.at[src], (lane, src)
-        ).wait_recv()
-    )
+    for part in range(parts):
+        cut = pl.ds(part * 8, 8)
+        spread(
+            lambda src: remote(
+                out2.at[src, :, cut], in2.at[src, :, cut],
+                s2.at[part, src], r2.at[part, src], (lane, src),
+            ).wait_recv()
+        )
 
     def finish(plane, carry):
         pair = in2[:, plane].reshape(width_x, pair_y)
@@ -473,12 +496,21 @@
 
     lax.fori_loop(0, local_depth, finish, 0)
 
-    def drain(dst):
-        remote(out1.at[dst], in1.at[me], s1.at[dst], r1.at[me], (lane, dst)).wait_send()
-        remote(miss.at[me], miss.at[me], sm.at[dst], rm.at[me], (lane, dst)).wait_send()
-        remote(out2.at[dst], in2.at[me], s2.at[dst], r2.at[me], (lane, dst)).wait_send()
-
-    spread(drain)
+    def drain(part, dst):
+        cut = pl.ds(part * 8, 8)
+        who = (lane, dst)
+        remote(
+            out1.at[dst, :, cut], in1.at[me, :, cut], s1.at[part, dst], r1.at[part, me], who
+        ).wait_send()
+        remote(
+            miss.at[me, cut], miss.at[me, cut], sm.at[part, dst], rm.at[part, me], who
+        ).wait_send()
+        remote(
+            out2.at[dst, :, cut], in2.at[me, :, cut], s2.at[part, dst], r2.at[part, me], who
+        ).wait_send()
+
+    for part in range(parts):
+        spread(lambda dst: drain(part, dst))
 
 
 def fused(incident, field_now, contrast, green_spectrum, detector_data):
@@ -490,11 +522,10 @@
     cos_x, sin_x = host_tables(width_x)
     cos_y, sin_y = host_tables(width_y)
     cos_z, sin_z = host_tables(depth)
-    xh, xl = host_split(np.concatenate([cos_x, sin_x], axis=0))
-    yfh, yfl = host_split(np.block([[cos_y, -sin_y], [sin_y, cos_y]]))
-    yih, yil = host_split(np.block([[cos_y, sin_y], [-sin_y, cos_y]]))
-    zh, zl = host_split(np.concatenate([cos_z, sin_z], axis=0))
-    zt = np.concatenate([zh, zh, zl], axis=1)
+    table_x = np.concatenate([cos_x, sin_x], axis=0).astype(np.float32)
+    forward_y = np.block([[cos_y, -sin_y], [sin_y, cos_y]]).astype(np.float32)
+    inverse_y = np.block([[cos_y, sin_y], [-sin_y, cos_y]]).astype(np.float32)
+    table_z = np.concatenate([cos_z, sin_z], axis=0).astype(np.float32)
     step = host_propagator(1, width_x, width_y)
     nearest = [depth - (s * local_depth + local_depth - 1) for s in range(slabs)]
     start = np.stack([host_propagator(d, width_x, width_y) for d in nearest])
@@ -504,7 +535,9 @@
     planes = pltpu.VMEM((local_depth, width_x, width_y), f32)
     padded = pltpu.VMEM((local_depth + 2 * passes, width_x, width_y), f32)
     turned = pltpu.VMEM((cols_x, depth, pair_y), f32)
-    several = pltpu.SemaphoreType.DMA((slabs,))
+    cols_table = pltpu.VMEM((pair_y, pair_y), jnp.bfloat16)
+    rows_table = pltpu.VMEM((2 * width_x, width_x), jnp.bfloat16)
+    several = pltpu.SemaphoreType.DMA((cols_x // 8, slabs))
     return pl.pallas_call(
         fused_kernel,
         out_shape=(
@@ -512,7 +545,7 @@
             jax.ShapeDtypeStruct(detector_data.shape, f32),
             jax.ShapeDtypeStruct(contrast.shape, f32),
         ),
-        in_specs=[vmem] * 11 + [anywhere] * 3,
+        in_specs=[anywhere] * 11,
         out_specs=(vmem, vmem, vmem),
         scratch_shapes=[
             block, block, block, block,
@@ -520,10 +553,20 @@
             planes, planes, padded, padded, turned, turned,
             pltpu.VMEM((width_x, pair_y), f32),
             pltpu.VMEM((width_x, width_y), f32),
-            pltpu.VMEM(incident.shape, jnp.bfloat16),
+            pltpu.VMEM(field_now.shape, f32),
+            planes,
+            pltpu.VMEM(forward_y.shape, f32),
+            pltpu.VMEM(table_x.shape, f32),
             pltpu.VMEM(green_spectrum.shape, f32),
             pltpu.VMEM((width_x, pair_y), f32),
-            pltpu.SemaphoreType.DMA((3,)),
+            pltpu.VMEM(detector_data.shape, f32),
+            pltpu.VMEM(table_z.shape, f32),
+            pltpu.VMEM((width_x, pair_y), f32),
+            pltpu.VMEM(inverse_y.shape, f32),
+            pltpu.VMEM(incident.shape, jnp.bfloat16),
+            cols_table, cols_table, cols_table, cols_table, rows_table, rows_table,
+            pltpu.VMEM((2 * depth, 4 * depth), jnp.bfloat16),
+            pltpu.SemaphoreType.DMA((11,)),
             several, several, several, several, several, several,
             pltpu.SemaphoreType.DMA((local_depth,)),
             pltpu.SemaphoreType.DMA((local_depth,)),
@@ -531,11 +574,11 @@
             pltpu.SemaphoreType.DMA((2,)),
         ],
         compiler_params=pltpu.CompilerParams(
-            collective_id=0, has_side_effects=True, vmem_limit_bytes=48 * 2**20
+            collective_id=0, has_side_effects=True, vmem_limit_bytes=60 * 2**20
         ),
     )(
-        field_now, contrast, detector_data, xh, xl, yfh, yfl, yih, yil, zt, step,
-        incident, green_spectrum, start,
+        field_now, contrast, forward_y, table_x, green_spectrum, step,
+        detector_data, table_z, start, inverse_y, incident,
     )
 
 

time: 91.2 us -> 98.2 us (1.077)
  Pallas kernels: 75.1 us -> 91.9 us
  local copies, waits for them, and re-layouts: 14.9 us -> 5.46 us
    pallas_call x1, Pallas kernels: 75.1 us -> 91.9 us  [fused(): pl.pallas_call(fused_kernel, out_shape=(jax.ShapeDtypeStruct(field_now.sh...]
    unnamed x29 -> x3, local copies, waits for them, and re-layouts: 14.9 us -> 5.46 us
where the time goes in v1:
time: 98.2 us; the launch traced here: 98 us
  Pallas kernels  91.9 us (94%)
  local copies, waits for them, and re-layouts  5.46 us (6%)
    pallas_call x1, Pallas kernels, fused(): pl.pallas_call(fused_kernel, out_shape=(jax.ShapeDtypeStruct(field_now.sh...  91.9 us
    unnamed x3, local copies, waits for them, and re-layouts  5.46 us

profile of v1, /device:TPU:9, one launch (start us, length us, event | category | flops | bytes accessed | tf_op | source)
XLA Modules:
  0.0 98.0 jit_solution(1150256878924019391)
XLA Ops:
  0.6 91.9 %shard_map.130 = (f32[1,2,4,256,128]{4,3,2,1,0:T(8,128)}, f32[1,2,16,128]{3,2,1,0:T(8,128)}, f32[4,256,128]{2,1,0:T(8,128)}) custom-call(f32[1,2,4,256,128]{4,3,2,1,0:T(8,128)} %field_any.1, f32[4,256,128]{2,1,0:T(8,128)} %contrast_any.1, f32[256,256]{1,0:T(8,128)} %constant.12.clone.yf_any, f32[512,256]{1,0:T(8,128)} %constant.13.clone.x_any, ...), custom_call_target="tpu_custom_call" | custom-call | tf_op jit(solution)/shard_map/pallas_call | solution.py:541
  92.5 2.3 %copy.17 = f32[1,2,4,256,128]{4,3,2,1,0:T(8,128)} copy(f32[1,2,4,256,128]{4,3,2,1,0:T(8,128)} %get-tuple-element.6) | data formatting | bytes 2097152
  94.8 1.3 %copy.18 = f32[1,2,16,128]{3,2,1,0:T(8,128)} copy(f32[1,2,16,128]{3,2,1,0:T(8,128)} %get-tuple-element.7) | data formatting | bytes 32768
  96.1 1.9 %copy.19 = f32[4,256,128]{2,1,0:T(8,128)} copy(f32[4,256,128]{2,1,0:T(8,128)} %get-tuple-element.8) | data formatting | bytes 1048576

commit v2 on v1

--- a/solution.py
+++ b/solution.py
@@ -280,12 +280,12 @@
         load.wait()
     yfh[...], yfl[...] = split_halves(yf[...])
     xh[...], xl[...] = split_halves(xt[...])
-    parts = cols_x // 8
+    parts = 1
     groups = math.gcd(local_depth, 2)
     size = local_depth // groups
 
     def send_block(part, first, count):
-        planes, rows = pl.ds(first, count), pl.ds(part * 8, 8)
+        planes, rows = pl.ds(first, count), pl.ds(0, cols_x)
         spread(
             lambda dst: remote(
                 out1.at[dst, planes, rows], in1.at[me, planes, rows],
@@ -328,14 +328,14 @@
         return carry
 
     for part in range(parts):
-        rows, cut = slice(part * 8, part * 8 + 8), pl.ds(part * 8, 8)
+        rows, cut = slice(0, cols_x), pl.ds(0, cols_x)
         spread(
             lambda src: remote(
                 out1.at[src, :, cut], in1.at[src, :, cut],
                 s1.at[part, src], r1.at[part, src], (lane, src),
             ).wait_recv()
         )
-        own = pl.ds(pl.multiple_of(me * cols_x + part * 8, 8), 8)
+        own = pl.ds(pl.multiple_of(me * cols_x, 8), cols_x)
         step_r, step_i = step_ref[own, :width_y], step_ref[own, width_y:]
 
         def horner(src, carry):
@@ -346,7 +346,7 @@
                 real, imag = (real * step_r - imag * step_i, real * step_i + imag * step_r)
             return real, imag
 
-        zero = jnp.zeros((8, width_y), jnp.float32)
+        zero = jnp.zeros((cols_x, width_y), jnp.float32)
         real, imag = lax.fori_loop(0, slabs, horner, (zero, zero))
         real = real / root_depth - detector[0, 0, rows]
         imag = imag / root_depth - detector[0, 1, rows]
@@ -360,11 +360,15 @@
                 sm.at[part, dst], rm.at[part, me], (lane, dst),
             ).start()
         )
-        block = in1[:, :, rows, :].reshape(depth, 8, pair_y)
-        zbuf[rows] = jnp.transpose(block, (1, 0, 2))
-        lax.fori_loop(part * 8, part * 8 + 8, convolve, 0)
-        block = jnp.transpose(zbuf[rows], (1, 0, 2))
-        out2[:, :, rows, :] = block.reshape(slabs, local_depth, 8, pair_y)
+        for first in range(0, cols_x, 8):
+            eight = slice(first, first + 8)
+            block = in1[:, :, eight, :].reshape(depth, 8, pair_y)
+            zbuf[eight] = jnp.transpose(block, (1, 0, 2))
+        lax.fori_loop(0, cols_x, convolve, 0)
+        for first in range(0, cols_x, 8):
+            eight = slice(first, first + 8)
+            block = jnp.transpose(zbuf[eight], (1, 0, 2))
+            out2[:, :, eight, :] = block.reshape(slabs, local_depth, 8, pair_y)
         spread(
             lambda dst: remote(
                 out2.at[dst, :, cut], in2.at[me, :, cut],
@@ -374,7 +378,7 @@
     in2[me] = out2[me]
 
     for part in range(parts):
-        cut = pl.ds(part * 8, 8)
+        cut = pl.ds(0, cols_x)
         spread(
             lambda src: remote(
                 miss.at[src, cut], miss.at[src, cut],
@@ -478,7 +482,7 @@
         lax.fori_loop(turn + 1, planes - 1 - turn, one, 0)
 
     for part in range(parts):
-        cut = pl.ds(part * 8, 8)
+        cut = pl.ds(0, cols_x)
         spread(
             lambda src: remote(
                 out2.at[src, :, cut], in2.at[src, :, cut],
@@ -497,7 +501,7 @@
     lax.fori_loop(0, local_depth, finish, 0)
 
     def drain(part, dst):
-        cut = pl.ds(part * 8, 8)
+        cut = pl.ds(0, cols_x)
         who = (lane, dst)
         remote(
             out1.at[dst, :, cut], in1.at[me, :, cut], s1.at[part, dst], r1.at[part, me], who
@@ -537,7 +541,7 @@
     turned = pltpu.VMEM((cols_x, depth, pair_y), f32)
     cols_table = pltpu.VMEM((pair_y, pair_y), jnp.bfloat16)
     rows_table = pltpu.VMEM((2 * width_x, width_x), jnp.bfloat16)
-    several = pltpu.SemaphoreType.DMA((cols_x // 8, slabs))
+    several = pltpu.SemaphoreType.DMA((1, slabs))
     return pl.pallas_call(
         fused_kernel,
         out_shape=(

time: 98.2 us -> 84.2 us (0.86)
  Pallas kernels: 91.9 us -> 77.3 us
    pallas_call x1, Pallas kernels: 91.9 us -> 77.3 us  [fused(): pl.pallas_call(fused_kernel, out_shape=(jax.ShapeDtypeStruct(field_now.sh...]
where the time goes in v2:
time: 84.2 us; the launch traced here: 83.4 us
  Pallas kernels  77.3 us (92%)
  local copies, waits for them, and re-layouts  5.46 us (6%)
    pallas_call x1, Pallas kernels, fused(): pl.pallas_call(fused_kernel, out_shape=(jax.ShapeDtypeStruct(field_now.sh...  77.3 us
    unnamed x3, local copies, waits for them, and re-layouts  5.46 us

profile of v2, /device:TPU:9, one launch (start us, length us, event | category | flops | bytes accessed | tf_op | source)
XLA Modules:
  0.0 83.4 jit_solution(11100849939652048940)
XLA Ops:
  0.6 77.3 %shard_map.130 = (f32[1,2,4,256,128]{4,3,2,1,0:T(8,128)}, f32[1,2,16,128]{3,2,1,0:T(8,128)}, f32[4,256,128]{2,1,0:T(8,128)}) custom-call(f32[1,2,4,256,128]{4,3,2,1,0:T(8,128)} %field_any.1, f32[4,256,128]{2,1,0:T(8,128)} %contrast_any.1, f32[256,256]{1,0:T(8,128)} %constant.12.clone.yf_any, f32[512,256]{1,0:T(8,128)} %constant.13.clone.x_any, ...), custom_call_target="tpu_custom_call" | custom-call | tf_op jit(solution)/shard_map/pallas_call | solution.py:545
  77.9 2.3 %copy.17 = f32[1,2,4,256,128]{4,3,2,1,0:T(8,128)} copy(f32[1,2,4,256,128]{4,3,2,1,0:T(8,128)} %get-tuple-element.6) | data formatting | bytes 2097152
  80.2 1.3 %copy.18 = f32[1,2,16,128]{3,2,1,0:T(8,128)} copy(f32[1,2,16,128]{3,2,1,0:T(8,128)} %get-tuple-element.7) | data formatting | bytes 32768
  81.5 1.9 %copy.19 = f32[4,256,128]{2,1,0:T(8,128)} copy(f32[4,256,128]{2,1,0:T(8,128)} %get-tuple-element.8) | data formatting | bytes 1048576

commit v3 on v2

--- a/solution.py
+++ b/solution.py
@@ -220,10 +220,10 @@
 
 def fused_kernel(
     field_any, contrast_any, yf_any, x_any, green_any, step_any,
-    detector_any, z_any, start_any, yi_any, incident_any,
+    detector_any, z_any, start_any, yi_any,
     field_out, misfit_out, contrast_out,
     out1, in1, out2, in2, miss, gmine, gpeer, cube, cube2, zbuf, gbuf, rbuf, fz,
-    field, contrast, yf, xt, green, step_ref, detector, zf, start, yi, inc,
+    field, contrast, yf, xt, green, step_ref, detector, zf, start, yi,
     yfh, yfl, yih, yil, xh, xl, zt_ref,
     load_sem, s1, r1, s2, r2, sm, rm, sg, rg, sh, rh,
 ):
@@ -249,9 +249,9 @@
 
     sources = [
         field_any, contrast_any, yf_any, x_any, green_any, step_any,
-        detector_any, z_any, start_any.at[me], yi_any, incident_any,
+        detector_any, z_any, start_any.at[me], yi_any,
     ]
-    held = [field, contrast, yf, xt, green, step_ref, detector, zf, start, yi, inc]
+    held = [field, contrast, yf, xt, green, step_ref, detector, zf, start, yi]
     early = 4
     loads = [
         pltpu.make_async_copy(src, dst, load_sem.at[i])
@@ -348,10 +348,12 @@
 
         zero = jnp.zeros((cols_x, width_y), jnp.float32)
         real, imag = lax.fori_loop(0, slabs, horner, (zero, zero))
-        real = real / root_depth - detector[0, 0, rows]
-        imag = imag / root_depth - detector[0, 1, rows]
+        real = real / root_depth
+        imag = imag / root_depth
         misfit_out[0, 0, rows] = real
         misfit_out[0, 1, rows] = imag
+        real = real - detector[0, 0, rows]
+        imag = imag - detector[0, 1, rows]
         miss[me, rows, :width_y] = real
         miss[me, rows, width_y:] = imag
         spread(
@@ -438,6 +440,25 @@
     @pl.when(me == slabs - 1)
     def _():
         cube[high_side] = jnp.zeros((passes, width_x, width_y), jnp.float32)
+
+    for part in range(parts):
+        cut = pl.ds(0, cols_x)
+        spread(
+            lambda src: remote(
+                out2.at[src, :, cut], in2.at[src, :, cut],
+                s2.at[part, src], r2.at[part, src], (lane, src),
+            ).wait_recv()
+        )
+
+    def finish(plane, carry):
+        pair = in2[:, plane].reshape(width_x, pair_y)
+        pair = transform_rows(pair, xh, xl, 1.0)
+        pair = transform_cols(pair, yih, yil)
+        field_out[0, 0, plane] = pair[:, :width_y]
+        field_out[0, 1, plane] = pair[:, width_y:]
+        return carry
+
+    lax.fori_loop(0, local_depth, finish, 0)
 
     pl.when(has_up)(up.wait_send)
     pl.when(has_down)(down.wait_send)
@@ -471,7 +492,7 @@
 
         def write(plane, value, turn=turn, target=target):
             if turn == passes - 1:
-                contrast_out[plane - passes] = value
+                contrast_out[plane - passes] = 2.0 * value
             else:
                 target[plane] = value
 
@@ -480,25 +501,6 @@
             return carry
 
         lax.fori_loop(turn + 1, planes - 1 - turn, one, 0)
-
-    for part in range(parts):
-        cut = pl.ds(0, cols_x)
-        spread(
-            lambda src: remote(
-                out2.at[src, :, cut], in2.at[src, :, cut],
-                s2.at[part, src], r2.at[part, src], (lane, src),
-            ).wait_recv()
-        )
-
-    def finish(plane, carry):
-        pair = in2[:, plane].reshape(width_x, pair_y)
-        pair = transform_rows(pair, xh, xl, 1.0)
-        pair = transform_cols(pair, yih, yil)
-        field_out[0, 0, plane] = inc[0, 0, plane].astype(jnp.float32) + pair[:, :width_y]
-        field_out[0, 1, plane] = inc[0, 1, plane].astype(jnp.float32) + pair[:, width_y:]
-        return carry
-
-    lax.fori_loop(0, local_depth, finish, 0)
 
     def drain(part, dst):
         cut = pl.ds(0, cols_x)
@@ -542,14 +544,14 @@
     cols_table = pltpu.VMEM((pair_y, pair_y), jnp.bfloat16)
     rows_table = pltpu.VMEM((2 * width_x, width_x), jnp.bfloat16)
     several = pltpu.SemaphoreType.DMA((1, slabs))
-    return pl.pallas_call(
+    scattered, predicted, doubled = pl.pallas_call(
         fused_kernel,
         out_shape=(
             jax.ShapeDtypeStruct(field_now.shape, f32),
             jax.ShapeDtypeStruct(detector_data.shape, f32),
             jax.ShapeDtypeStruct(contrast.shape, f32),
         ),
-        in_specs=[anywhere] * 11,
+        in_specs=[anywhere] * 10,
         out_specs=(vmem, vmem, vmem),
         scratch_shapes=[
             block, block, block, block,
@@ -567,10 +569,9 @@
             pltpu.VMEM(table_z.shape, f32),
             pltpu.VMEM((width_x, pair_y), f32),
             pltpu.VMEM(inverse_y.shape, f32),
-            pltpu.VMEM(incident.shape, jnp.bfloat16),
             cols_table, cols_table, cols_table, cols_table, rows_table, rows_table,
             pltpu.VMEM((2 * depth, 4 * depth), jnp.bfloat16),
-            pltpu.SemaphoreType.DMA((11,)),
+            pltpu.SemaphoreType.DMA((10,)),
             several, several, several, several, several, several,
             pltpu.SemaphoreType.DMA((local_depth,)),
             pltpu.SemaphoreType.DMA((local_depth,)),
@@ -582,8 +583,10 @@
         ),
     )(
         field_now, contrast, forward_y, table_x, green_spectrum, step,
-        detector_data, table_z, start, inverse_y, incident,
-    )
+        detector_data, table_z, start, inverse_y,
+    )
+    field_next = incident.astype(f32) + scattered
+    return (field_next, predicted - detector_data, 0.5 * doubled)
 
 
 def whole_tiles(mesh, arrays):

time: 84.2 us -> 81.2 us (0.964)
  other arithmetic: 0 us -> 5.48 us
  local copies, waits for them, and re-layouts: 5.46 us -> 0.01 us
  Pallas kernels: 77.3 us -> 74.2 us
    unnamed x3 -> x4, local copies, waits for them, and re-layouts: 5.46 us -> 0.01 us
    pallas_call x1, Pallas kernels: 77.3 us -> 74.2 us  [fused(): pl.pallas_call(fused_kernel, out_shape=(jax.ShapeDtypeStruct(field_now.sh...]
    add x0 -> x1, other arithmetic: none -> 2.29 us  [fused(): field_next = incident.astype(f32) + scattered]
    mul x0 -> x1, other arithmetic: none -> 1.87 us  [fused(): return (field_next, predicted - detector_data, 0.5 * doubled)]
    sub x0 -> x1, other arithmetic: none -> 1.33 us  [fused(): return (field_next, predicted - detector_data, 0.5 * doubled)]
where the time goes in v3:
time: 81.2 us; the launch traced here: 80.3 us
  Pallas kernels  74.2 us (91%)
  other arithmetic  5.48 us (7%)
    pallas_call x1, Pallas kernels, fused(): pl.pallas_call(fused_kernel, out_shape=(jax.ShapeDtypeStruct(field_now.sh...  74.2 us
    add x1, other arithmetic, fused(): field_next = incident.astype(f32) + scattered  2.29 us
    mul x1, other arithmetic, fused(): return (field_next, predicted - detector_data, 0.5 * doubled)  1.87 us

profile of v3, /device:TPU:9, one launch (start us, length us, event | category | flops | bytes accessed | tf_op | source)
XLA Modules:
  0.0 80.3 jit_solution(3713451436454917848)
XLA Ops:
  0.6 0.0 copy-start.1
  0.6 0.0 copy-start
  0.7 74.2 %shard_map.130 = (f32[1,2,4,256,128]{4,3,2,1,0:T(8,128)}, f32[1,2,16,128]{3,2,1,0:T(8,128)}, f32[4,256,128]{2,1,0:T(8,128)}) custom-call(f32[1,2,4,256,128]{4,3,2,1,0:T(8,128)} %field_any.1, f32[4,256,128]{2,1,0:T(8,128)} %contrast_any.1, f32[256,256]{1,0:T(8,128)} %constant.14.clone.yf_any, f32[512,256]{1,0:T(8,128)} %constant.15.clone.x_any, ...), custom_call_target="tpu_custom_call" | custom-call | tf_op jit(solution)/shard_map/pallas_call | solution.py:547
  74.9 0.0 copy-done
  74.9 2.3 %convert_add_fusion = f32[1,2,4,256,128]{4,3,2,1,0:T(8,128)} fusion(f32[1,2,4,256,128]{4,3,2,1,0:T(8,128)} %get-tuple-element.6, bf16[1,2,4,256,128]{4,3,2,1,0:T(8,128)(2,1)S(1)} %copy-done), kind=kLoop, calls=%fused_computation | loop fusion | flops 524288 | bytes 2621440 | tf_op jit(solution)/shard_map/add | solution.py:588
  77.1 0.0 copy-done.1
  77.2 1.3 %sub.3 = f32[1,2,16,128]{3,2,1,0:T(8,128)} subtract(f32[1,2,16,128]{3,2,1,0:T(8,128)} %get-tuple-element.7, f32[1,2,16,128]{3,2,1,0:T(8,128)S(1)} %copy-done.1) | non-fusion elementwise | flops 4096 | bytes 49152 | tf_op jit(solution)/shard_map/sub | solution.py:589
  78.5 1.9 %broadcast_multiply_fusion = f32[4,256,128]{2,1,0:T(8,128)} fusion(f32[4,256,128]{2,1,0:T(8,128)} %get-tuple-element.8), kind=kLoop, calls=%fused_computation.1 | loop fusion | flops 131072 | bytes 1048576 | tf_op jit(solution)/shard_map/mul | solution.py:589
Async XLA Ops:
  0.6 76.5 %copy-start.1 = (f32[1,2,16,128]{3,2,1,0:T(8,128)S(1)}, f32[1,2,16,128]{3,2,1,0:T(8,128)}, u32[]{:S(2)}) copy-start(f32[1,2,16,128]{3,2,1,0:T(8,128)} %detector_any.1) | copy-start | bytes 49156
  0.6 74.2 %copy-start = (bf16[1,2,4,256,128]{4,3,2,1,0:T(8,128)(2,1)S(1)}, bf16[1,2,4,256,128]{4,3,2,1,0:T(8,128)(2,1)}, u32[]{:S(2)}) copy-start(bf16[1,2,4,256,128]{4,3,2,1,0:T(8,128)(2,1)} %param.11) | copy-start | bytes 1572868

commit v4 on v3

--- a/solution.py
+++ b/solution.py
@@ -239,8 +239,11 @@
     def at(hop):
         return lax.rem(me + hop, slabs)
 
+    def far_first(hop):
+        return lax.rem(hop + slabs // 2 - 1, slabs - 1) + 1
+
     def spread(body):
-        lax.fori_loop(1, slabs, lambda hop, carry: (body(at(hop)), carry)[1], 0)
+        lax.fori_loop(1, slabs, lambda hop, carry: (body(at(far_first(hop))), carry)[1], 0)
 
     barrier = pltpu.get_barrier_semaphore()
 

time: 81.2 us -> 79.8 us (0.983)
  Pallas kernels: 74.2 us -> 72.8 us
    pallas_call x1, Pallas kernels: 74.2 us -> 72.8 us  [fused(): pl.pallas_call(fused_kernel, out_shape=(jax.ShapeDtypeStruct(field_now.sh...]
where the time goes in v4:
time: 79.8 us; the launch traced here: 78.9 us
  Pallas kernels  72.8 us (91%)
  other arithmetic  5.48 us (7%)
    pallas_call x1, Pallas kernels, fused(): pl.pallas_call(fused_kernel, out_shape=(jax.ShapeDtypeStruct(field_now.sh...  72.8 us
    add x1, other arithmetic, fused(): field_next = incident.astype(f32) + scattered  2.29 us
    mul x1, other arithmetic, fused(): return (field_next, predicted - detector_data, 0.5 * doubled)  1.87 us

profile of v4, /device:TPU:9, one launch (start us, length us, event | category | flops | bytes accessed | tf_op | source)
XLA Modules:
  0.0 78.9 jit_solution(15308864281542085305)
XLA Ops:
  0.6 0.0 copy-start.1
  0.6 0.0 copy-start
  0.7 72.8 %shard_map.130 = (f32[1,2,4,256,128]{4,3,2,1,0:T(8,128)}, f32[1,2,16,128]{3,2,1,0:T(8,128)}, f32[4,256,128]{2,1,0:T(8,128)}) custom-call(f32[1,2,4,256,128]{4,3,2,1,0:T(8,128)} %field_any.1, f32[4,256,128]{2,1,0:T(8,128)} %contrast_any.1, f32[256,256]{1,0:T(8,128)} %constant.14.clone.yf_any, f32[512,256]{1,0:T(8,128)} %constant.15.clone.x_any, ...), custom_call_target="tpu_custom_call" | custom-call | tf_op jit(solution)/shard_map/pallas_call | solution.py:550
  73.4 0.0 copy-done
  73.5 2.3 %convert_add_fusion = f32[1,2,4,256,128]{4,3,2,1,0:T(8,128)} fusion(f32[1,2,4,256,128]{4,3,2,1,0:T(8,128)} %get-tuple-element.6, bf16[1,2,4,256,128]{4,3,2,1,0:T(8,128)(2,1)S(1)} %copy-done), kind=kLoop, calls=%fused_computation | loop fusion | flops 524288 | bytes 2621440 | tf_op jit(solution)/shard_map/add | solution.py:591
  75.7 0.0 copy-done.1
  75.7 1.3 %sub.3 = f32[1,2,16,128]{3,2,1,0:T(8,128)} subtract(f32[1,2,16,128]{3,2,1,0:T(8,128)} %get-tuple-element.7, f32[1,2,16,128]{3,2,1,0:T(8,128)S(1)} %copy-done.1) | non-fusion elementwise | flops 4096 | bytes 49152 | tf_op jit(solution)/shard_map/sub | solution.py:592
  77.1 1.9 %broadcast_multiply_fusion = f32[4,256,128]{2,1,0:T(8,128)} fusion(f32[4,256,128]{2,1,0:T(8,128)} %get-tuple-element.8), kind=kLoop, calls=%fused_computation.1 | loop fusion | flops 131072 | bytes 1048576 | tf_op jit(solution)/shard_map/mul | solution.py:592
Async XLA Ops:
  0.6 75.1 %copy-start.1 = (f32[1,2,16,128]{3,2,1,0:T(8,128)S(1)}, f32[1,2,16,128]{3,2,1,0:T(8,128)}, u32[]{:S(2)}) copy-start(f32[1,2,16,128]{3,2,1,0:T(8,128)} %detector_any.1) | copy-start | bytes 49156
  0.6 72.8 %copy-start = (bf16[1,2,4,256,128]{4,3,2,1,0:T(8,128)(2,1)S(1)}, bf16[1,2,4,256,128]{4,3,2,1,0:T(8,128)(2,1)}, u32[]{:S(2)}) copy-start(bf16[1,2,4,256,128]{4,3,2,1,0:T(8,128)(2,1)} %param.11) | copy-start | bytes 1572868
